TPU v7x, 128 devices: a whole 4x4x4 slice. The times are simulated.
128 devices in a mesh: head: 4 (over x_lo, core), outer: 2 (over x_hi), inner: 16 (over z, y).
Axes of the slice: x: 4 (x_hi: 2, x_lo: 2; x = x_hi * 2 + x_lo), y: 4, z: 4, core: 2. Of those that a mesh axis runs over, the one named last changes fastest.
Arguments:
- queries: bfloat16 [8192, 8192], P(('outer', 'inner'), 'head'), may hold values from -128 to 128
- keys: bfloat16 [8192, 1024], P(('outer', 'inner'), 'head'), may hold values from -6 to 6
- values: bfloat16 [8192, 1024], P(('outer', 'inner'), 'head'), may hold values from -6 to 6
- segment_ids: int32 [8192], P(('outer', 'inner')), may hold values from 0 to 7, never falling along the last dimension, each value on 1 to 6144 neighbouring positions
- value_weight: float32 [8192], P('head'), may hold values from -0.3 to 0.3
- targets: float32 [8192], P(('outer', 'inner')), may hold values from -6 to 6
- upstream: bfloat16 [8192, 8192], P(('outer', 'inner'), 'head'), may hold values from -6 to 6
Outputs:
- query_grad: bfloat16 [8192, 8192], P(('outer', 'inner'), 'head')
- key_grad: bfloat16 [8192, 1024], P(('outer', 'inner'), 'head')
- value_grad: bfloat16 [8192, 1024], P(('outer', 'inner'), 'head')
- value_error: float32 [8192], P(('outer', 'inner'))
- readout_grad: float32 [8192], P('head')
Inputs may be any that keep to these rules, and one draw needn't show every extreme that they name: `segment_ids`: segment numbers never fall along the tokens; a segment holds at most 6144 tokens, and one holds exactly that many.
All inputs are finite; a program needn't handle non-finite values.
Results may differ from a plain program's by a relative error of at most 0.027.
Values may be sent and summed in bfloat16 or wider, within the bound.
No kernel may reach another device: no remote copies, remote signals or barrier semaphores. Data moves between devices by JAX's collectives and lax.ppermute only.
A program may use at most 448 MiB of HBM per device.

v0:
```python
import jax
import jax.numpy as jnp
from jax import lax
from jax.sharding import PartitionSpec as P

HD = 128
GROUP = 8


def local(queries, keys, values, segment_ids, value_weight, targets, upstream):
    tok_rows = queries.shape[0]
    heads_kv = keys.shape[1] // HD
    kv_width = heads_kv * HD
    score_scale = HD ** (-0.5)
    context = lax.axis_size(("outer", "inner"))
    seq_len = tok_rows * context
    first_row = lax.axis_index(("outer", "inner")) * tok_rows
    query_pos = first_row + jnp.arange(tok_rows, dtype=jnp.int32)
    query_heads = queries.reshape(tok_rows, heads_kv, GROUP, HD)

    def logits_of(key_rows, key_seg):
        key_pos = jnp.arange(key_rows.shape[0], dtype=jnp.int32)
        allowed = (
            (key_pos[None, :] <= query_pos[:, None])
            & (key_pos[None, :] >= 0)
            & (key_seg[None, :] == segment_ids[:, None])
        )
        logits = (
            jnp.einsum(
                "qhgd,khd->hgqk",
                query_heads,
                key_rows.reshape(-1, heads_kv, HD),
                preferred_element_type=jnp.float32,
            )
            * score_scale
        )
        return (logits, allowed)

    def guarded(compute, carried, key_seg, offset):
        active = (offset <= first_row + tok_rows - 1) & (key_seg[-1] >= segment_ids[0])
        return lax.cond(active, compute, lambda unchanged: unchanged, carried)

    def block_grads(grad_query, key_piece):
        key_rows, value_rows, key_seg = key_piece
        logits, allowed = logits_of(key_rows, key_seg)
        attn_prob = jnp.where(allowed, jnp.exp(logits - lse[..., None]), 0.0)
        prob_low = attn_prob.astype(jnp.bfloat16)
        key_heads = key_rows.reshape(-1, heads_kv, HD)
        value_heads = value_rows.reshape(-1, heads_kv, HD)
        dprob = jnp.einsum(
            "qhgd,khd->hgqk", dout_heads, value_heads, preferred_element_type=jnp.float32
        )
        dlogit = (attn_prob * (dprob - row_delta[..., None])).astype(jnp.bfloat16)
        grad_query = (
            jnp.einsum("hgqk,khd->qhgd", dlogit, key_heads, preferred_element_type=jnp.float32)
            * score_scale
        )
        grad_key = (
            jnp.einsum("hgqk,qhgd->khd", dlogit, query_heads, preferred_element_type=jnp.float32)
            * score_scale
        )
        grad_value = jnp.einsum(
            "hgqk,qhgd->khd", prob_low, dout_heads, preferred_element_type=jnp.float32
        )
        stacked = jnp.concatenate(
            [
                grad_key.reshape(key_rows.shape[0], kv_width),
                grad_value.reshape(key_rows.shape[0], kv_width),
            ],
            1,
        )
        return (grad_query, stacked)

    start_state = (
        jnp.full((heads_kv, GROUP, tok_rows), -1e30, jnp.float32),
        jnp.zeros((heads_kv, GROUP, tok_rows), jnp.float32),
        jnp.zeros((tok_rows, heads_kv, GROUP, HD), jnp.float32),
    )
    key_rows = lax.all_gather(keys, ("outer", "inner"), axis=0, tiled=True)
    value_rows = lax.all_gather(values, ("outer", "inner"), axis=0, tiled=True)
    key_seg = lax.all_gather(segment_ids, ("outer", "inner"), axis=0, tiled=True)

    def compute(state):
        running_max, totals, weighted = state
        logits, allowed = logits_of(key_rows, key_seg)
        new_max = jnp.maximum(running_max, jnp.max(jnp.where(allowed, logits, -1e30), -1))
        attn_prob = jnp.where(allowed, jnp.exp(logits - new_max[..., None]), 0.0)
        totals = jnp.sum(attn_prob, -1)
        value_heads = value_rows.reshape(-1, heads_kv, HD)
        mixed = jnp.einsum(
            "hgqk,khd->qhgd",
            attn_prob.astype(jnp.bfloat16),
            value_heads,
            preferred_element_type=jnp.float32,
        )
        weighted = mixed
        return (new_max, totals, weighted)

    forward = guarded(compute, start_state, key_seg, jnp.int32(0))
    running_max, totals, weighted = forward
    lse = running_max + jnp.log(totals)
    attn_out = (weighted / totals.transpose(2, 0, 1)[..., None]).astype(jnp.bfloat16)
    attn_flat = attn_out.reshape(tok_rows, -1).astype(jnp.float32)
    critic = lax.psum(jnp.sum(attn_flat * value_weight[None, :], -1), "head")
    value_error = critic - targets
    readout = lax.psum(jnp.sum(value_error[:, None] * attn_flat, 0), ("outer", "inner"))
    dout = (value_error[:, None] * value_weight[None, :] + upstream.astype(jnp.float32)).astype(
        jnp.bfloat16
    )
    dout_heads = dout.reshape(tok_rows, heads_kv, GROUP, HD)
    row_delta = jnp.sum(
        dout_heads.astype(jnp.float32) * attn_out.astype(jnp.float32), -1
    ).transpose(1, 2, 0)
    query_start = jnp.zeros((tok_rows, heads_kv, GROUP, HD), jnp.float32)
    grad_start = (query_start, jnp.zeros((seq_len, 2 * kv_width), jnp.float32))
    key_piece = (
        lax.all_gather(keys, ("outer", "inner"), axis=0, tiled=True),
        lax.all_gather(values, ("outer", "inner"), axis=0, tiled=True),
        lax.all_gather(segment_ids, ("outer", "inner"), axis=0, tiled=True),
    )

    def compute(state):
        grad_query, buffer = state
        grad_query, stacked = block_grads(grad_query, key_piece)
        return (grad_query, stacked)

    backward = guarded(compute, grad_start, key_piece[2], jnp.int32(0))
    grad_query, buffer = backward
    summed = lax.psum_scatter(
        buffer.astype(jnp.bfloat16), ("outer", "inner"), scatter_dimension=0, tiled=True
    ).astype(jnp.float32)
    query_grad = grad_query.reshape(tok_rows, -1).astype(jnp.bfloat16)
    key_grad = summed[:, :kv_width].astype(jnp.bfloat16)
    value_grad = summed[:, kv_width:].astype(jnp.bfloat16)
    return (query_grad, key_grad, value_grad, value_error, readout)


def solution(mesh):
    return jax.shard_map(
        local,
        mesh=mesh,
        in_specs=(
            P(("outer", "inner"), "head"),
            P(("outer", "inner"), "head"),
            P(("outer", "inner"), "head"),
            P(("outer", "inner")),
            P("head"),
            P(("outer", "inner")),
            P(("outer", "inner"), "head"),
        ),
        out_specs=(
            P(("outer", "inner"), "head"),
            P(("outer", "inner"), "head"),
            P(("outer", "inner"), "head"),
            P(("outer", "inner")),
            P("head"),
        ),
        check_vma=False,
    )
```

profile of v0, /device:TPU:0, one launch (start us, length us, event | category | flops | bytes accessed | tf_op | source)
XLA Modules:
  0.0 815.4 jit_solution(3327124168226559466)
XLA Ops:
  7.2 0.0 all-gather.6.cloned.1.call-start
  7.2 0.7 all-gather.6.cloned.1.call-update
  7.9 0.0 all-gather.4.cloned.1.call-start
  7.9 1.7 copy.40
  9.6 0.0 all-gather.4.cloned.1.call-update
  9.6 0.0 reduce-scatter.2.cloned.1.call-start
  9.7 1.2 slice.17
  10.9 96.7 %all-gather = s32[32,1,256]{2,1,0:T(1,128)S(1)} all-gather(s32[1,1,256]{2,1,0:T(1,128)} %bitcast.104), channel_id=1, replica_groups=mesh['head'=4,'outer'=2,'inner'=16] {'outer','inner'}, dimensions={0}, use_global_device_ids=true | all-gather | bytes 33792 | tf_op jit(solution)/shard_map/all_gather | solution.py:119
  107.6 0.6 slice.20
  109.5 1.5 copy.41
  110.9 0.6 iota_add_fusion
  111.5 0.0 all-gather.6.cloned.1.call-done
  111.5 62.7 %all-gather.4.cloned.1.call-done = bf16[8192,256]{0,1:T(8,128)(2,1)} async-done(((bf16[256,256]{0,1:T(8,128)(2,1)}), bf16[8192,256]{0,1:T(8,128)(2,1)}) %all-gather.4.cloned.1.call-update) | async-done | bytes 4194320 | tf_op jit(solution)/shard_map/all_gather | solution.py:117
  174.2 0.0 copy-start.4
  174.2 0.0 copy-start.9
  174.2 155.8 %conditional.2 = (f32[2,8,256]{2,1,0:T(8,128)}, f32[2,8,256]{2,1,0:T(8,128)}, f32[2,8,256]{2,1,0:T(8,128)S(1)}, f32[256,2,8,128]{0,3,2,1:T(8,128)}) conditional(s32[]{:T(128)} %convert_element_type.49, () %tuple.29, (s32[256]{0:T(256)}, s32[8192]{0:T(1024)S(1)}, s32[256]{0:T(256)}, bf16[8192,256]{0,1:T(8,128)(2,1)}, ...), branch_computations={%region_0.0_spmd, %region_1.4_spmd} | conditional | flops 17555255296 | bytes 435329088 | solution.py:41
  174.2 0.0 copy-start.7
  174.2 6.9 reshape.59
  181.1 0.0 copy-done.7
  181.1 4.4 fusion.8
  185.5 46.3 %fusion = (f32[2,8,256]{2,1,0:T(8,128)S(1)}, f32[2,8192,256,8]{2,1,3,0:T(8,128)}) fusion(pred[256,8192]{0,1:T(8,128)(4,1)S(1)} %fusion.8, bf16[8192,2,128,1]{0,2,3,1:T(8,128)(2,1)} %bitcast.88, bf16[256,2,8,128]{0,3,2,1:T(8,128)(2,1)S(1)} %get-tuple-element.83), kind=kOutput, calls=%fused_computation.2 | convolution fusion | flops 8690593792 | bytes 141574144 | tf_op jit(solution)/shard_map/cond/branch_1_fun/qhgd,khd->hgqk/dot_general | solution.py:29
  231.8 0.6 broadcast_maximum_fusion
  232.4 51.9 %fusion.10 = f32[256,2,8,128]{3,0,2,1:T(8,128)} fusion(bf16[8192,2,128,1]{2,1,0,3:T(2,128)(2,1)} %bitcast.94, f32[2,8192,256,8]{2,1,3,0:T(8,128)} %get-tuple-element.97, f32[2,8,256]{2,1,0:T(8,128)} %broadcast_maximum_fusion, pred[256,8192]{0,1:T(8,128)(4,1)S(1)} %fusion.8), kind=kOutput, calls=%fused_computation.12 | convolution fusion | flops 8724152320 | bytes 142622720 | tf_op jit(solution)/shard_map/cond/branch_1_fun/hgqk,khd->qhgd/dot_general | solution.py:90
  284.3 42.0 %fusion.4 = f32[2,8,256]{2,1,0:T(8,128)} fusion(f32[2,8192,256,8]{2,1,3,0:T(8,128)} %get-tuple-element.97, f32[2,8,256]{2,1,0:T(8,128)} %broadcast_maximum_fusion, pred[256,8192]{0,1:T(8,128)(4,1)S(1)} %fusion.8), kind=kLoop, calls=%fused_computation.6 | loop fusion | flops 134213632 | bytes 136347648 | tf_op jit(solution)/shard_map/cond/branch_1_fun/reduce_sum | solution.py:88
  326.3 2.9 copy.73
  329.2 0.7 log.5
  330.0 0.0 copy-start.2
  330.0 0.0 copy-start.6
  330.0 0.6 copy-done.2
  330.6 0.0 copy-done.4
  330.6 0.0 copy-start.3
  330.6 2.0 fusion.30
  332.5 6.1 psum.14
  338.7 0.0 copy-done.9
  338.7 0.0 copy-start.8
  338.7 2.5 add_convert_fusion
  341.2 1.5 copy.45
  342.7 1.1 fusion.32
  343.8 0.0 copy-done.6
  343.8 0.0 copy-done.3
  343.8 0.0 copy-done.8
  343.8 248.9 %conditional.3 = (bf16[8192,512]{0,1:T(8,128)(2,1)}, bf16[256,2048]{1,0:T(8,128)(2,1)}) conditional(s32[]{:T(128)} %convert_element_type.49, () %tuple.28, (s32[256]{0:T(256)}, s32[8192]{0:T(1024)S(1)}, s32[256]{0:T(256)S(1)}, bf16[8192,256]{0,1:T(8,128)(2,1)}, bf16[256,2,8,128]{0,3,2,1:T(8,128)(2,1)S(1)}, /*index=5*/f32[2,8,256]{2,1,0:T(8,128)}, ...), branch_computations={%region_7.8_spmd, %region_8.9_spmd} | conditional | flops 43313532928 | bytes 672270400 | solution.py:41
  343.8 0.0 copy-start
  343.8 0.7 add.22
  344.6 5.3 fusion.26
  349.9 6.9 reshape.62
  356.8 45.6 %fusion.34 = f32[2,8192,256,8]{2,1,3,0:T(8,128)} fusion(bf16[8192,2,128,1]{0,2,3,1:T(8,128)(2,1)} %bitcast.89, bf16[256,2,8,128]{0,3,2,1:T(8,128)(2,1)S(1)} %get-tuple-element.45), kind=kOutput, calls=%fused_computation.44 | convolution fusion | flops 8589934592 | bytes 139460608 | tf_op jit(solution)/shard_map/cond/branch_1_fun/qhgd,khd->hgqk/dot_general | solution.py:29
  402.4 0.0 copy-done
  402.4 46.7 %fusion.22 = bf16[2,8192,128,1]{1,2,3,0:T(8,128)(2,1)} fusion(bf16[256,2,8,128]{0,3,2,1:T(8,128)(2,1)S(1)} %get-tuple-element.49, f32[2,8192,256,8]{2,1,3,0:T(8,128)} %fusion.34, f32[2,8,256]{2,1,0:T(8,128)S(1)} %add.22, pred[256,8192]{0,1:T(8,128)(4,1)} %fusion.26), kind=kOutput, calls=%fused_computation.23 | convolution fusion | flops 8724152320 | bytes 141574144 | tf_op jit(solution)/shard_map/cond/branch_1_fun/hgqk,qhgd->khd/dot_general | solution.py:62
  449.1 79.6 %fusion.18 = bf16[2,8,256,8192]{2,3,1,0:T(8,128)(2,1)} fusion(f32[2,8192,256,8]{2,1,3,0:T(8,128)} %fusion.34, f32[2,8,256]{2,1,0:T(8,128)S(1)} %get-tuple-element.50, f32[2,8,256]{2,1,0:T(8,128)S(1)} %add.22, pred[256,8192]{0,1:T(8,128)(4,1)} %fusion.26, bf16[256,2,8,128]{0,3,2,1:T(8,128)(2,1)S(1)} %get-tuple-element.49, bf16[8192,2,128,1]{2,1,0,3:T(2,128)(2,1)} %bitcast.95), kind=kOutput, calls=%fused_computation.18 | convolution fusion | flops 8791261184 | bytes 208699392 | tf_op jit(solution)/shard_map/cond/branch_1_fun/qhgd,khd->hgqk/dot_general | solution.py:50
  528.7 0.0 copy-start.1
  528.7 24.1 %multiply_convert_fusion = bf16[2,8,256,128]{2,3,1,0:T(8,128)(2,1)S(1)} fusion(bf16[8192,2,128,1]{0,2,3,1:T(8,128)(2,1)} %bitcast.90, bf16[2,8,256,8192]{2,3,1,0:T(8,128)(2,1)} %fusion.18), kind=kOutput, calls=%fused_computation.31 | convolution fusion | flops 8590983168 | bytes 72351744 | tf_op jit(solution)/shard_map/cond/branch_1_fun/hgqk,khd->qhgd/dot_general | solution.py:55
  552.7 0.0 copy-done.1
  552.7 30.9 %fusion.25 = bf16[2,8192,128]{1,2,0:T(8,128)(2,1)} fusion(bf16[2,8,256,8192]{2,3,1,0:T(8,128)(2,1)} %fusion.18, bf16[256,2,8,128]{0,3,2,1:T(8,128)(2,1)S(1)} %copy-done.1), kind=kOutput, calls=%fused_computation.27 | convolution fusion | flops 8594128896 | bytes 72351744 | tf_op jit(solution)/shard_map/cond/branch_1_fun/hgqk,qhgd->khd/dot_general | solution.py:59
  583.6 1.4 copy.75
  585.0 7.7 pad_maximum_fusion
  592.7 12.0 %copy.46 = bf16[8192,512]{1,0:T(8,128)(2,1)} copy(bf16[8192,512]{0,1:T(8,128)(2,1)} %get-tuple-element.67) | data formatting | bytes 16777216 | tf_op jit(solution)/shard_map/cond | solution.py:41
  604.7 0.0 copy-start.5
  604.7 0.0 reduce-scatter.2.cloned.1.call-update
  604.7 0.7 copy-done.5
  605.4 95.9 %psum.15 = f32[2048]{0:T(1024)} all-reduce(f32[2048]{0:T(1024)S(1)} %bitcast.102), channel_id=1, replica_groups=mesh['head'=4,'outer'=2,'inner'=16] {'outer','inner'}, use_global_device_ids=true, to_apply=%region_11.12 | all-reduce | flops 2048 | bytes 16384 | tf_op jit(solution)/shard_map/psum | solution.py:106
  701.3 105.9 %reduce-scatter.2.cloned.1.call-done = bf16[256,512]{1,0:T(8,128)(2,1)} async-done(((bf16[8192,512]{1,0:T(8,128)(2,1)}), bf16[256,512]{1,0:T(8,128)(2,1)}) %reduce-scatter.2.cloned.1.call-update) | async-done | bytes 262160 | tf_op jit(solution)/shard_map/reduce_scatter | solution.py:129
  807.2 1.7 fusion.33
  (1 shorter events, 0.0 us)
Async XLA Ops:
  7.2 104.3 %all-gather.6.cloned.1.call-start = ((), (), s32[]{:S(2)}) async-start(), calls=%async_computation.2 | async-start | bytes 4325376 | tf_op jit(solution)/shard_map/all_gather | solution.py:80
  7.9 166.3 %all-gather.4.cloned.1.call-start = ((), (), s32[]{:S(2)}) async-start(), calls=%async_computation.1 | async-start | bytes 4325376 | tf_op jit(solution)/shard_map/all_gather | solution.py:117
  9.6 797.6 %reduce-scatter.2.cloned.1.call-start = ((), (), s32[]{:S(2)}) async-start(), calls=%async_computation.3 | async-start | bytes 8650752 | tf_op jit(solution)/shard_map/reduce_scatter | solution.py:129
  174.2 156.4 %copy-start.4 = (f32[2048]{0:T(1024)S(1)}, f32[2048]{0:T(1024)}, u32[]{:S(2)}) copy-start(f32[2048]{0:T(1024)} %param.15) | copy-start | bytes 24580
  174.2 164.5 %copy-start.9 = (f32[256]{0:T(256)S(1)}, f32[256]{0:T(256)}, u32[]{:S(2)}) copy-start(f32[256]{0:T(256)} %param.16) | copy-start | bytes 3076
  174.2 6.9 copy-start.7
  330.0 0.6 copy-start.2
  330.0 13.8 %copy-start.6 = (s32[256]{0:T(256)S(1)}, s32[256]{0:T(256)}, u32[]{:S(2)}) copy-start(s32[256]{0:T(256)} %param.14) | copy-start | bytes 3076
  330.6 13.2 %copy-start.3 = (f32[2,8,256]{2,1,0:T(8,128)S(1)}, f32[2,8,256]{2,1,0:T(8,128)}, u32[]{:S(2)}) copy-start(f32[2,8,256]{2,1,0:T(8,128)} %copy-done.2) | copy-start | bytes 49156
  338.7 5.1 copy-start.8
  343.8 58.6 %copy-start = (bf16[256,2,8,128]{0,3,2,1:T(8,128)(2,1)}, bf16[256,2,8,128]{0,3,2,1:T(8,128)(2,1)S(1)}, u32[]{:S(2)}) copy-start(bf16[256,2,8,128]{0,3,2,1:T(8,128)(2,1)S(1)} %get-tuple-element.45) | copy-start | bytes 3145732 | tf_op jit(solution)/shard_map/cond
  528.7 24.1 %copy-start.1 = (bf16[256,2,8,128]{0,3,2,1:T(8,128)(2,1)S(1)}, bf16[256,2,8,128]{0,3,2,1:T(8,128)(2,1)}, u32[]{:S(2)}) copy-start(bf16[256,2,8,128]{0,3,2,1:T(8,128)(2,1)} %copy-done) | copy-start | bytes 3145732 | tf_op jit(solution)/shard_map/cond
  604.7 0.7 copy-start.5
Sparse Core Ops, SparseCore 0:
  11.1 82.9 all-gather.5
  97.4 76.6 all-gather.3
  604.8 202.3 reduce-scatter.1
where the time goes:
time: 817 us; the launch traced here: 815 us
  matrix products  325 us (40%)
  blocking collectives  199 us (24%)
  waiting for transfers between devices  169 us (21%)
  other arithmetic  66.9 us (8%)
  local copies, waits for them, and re-layouts  40.3 us (5%)
  between operations  15.1 us (2%)
    reduce_scatter x1, waiting for transfers between devices, local(): lax.psum_scatter(buffer.astype(jnp.bfloat16), ('outer', 'inner'), scatter...  106 us
    all_gather x1, blocking collectives, local(): lax.all_gather(segment_ids, ('outer', 'inner'), axis=0, tiled=True)  96.7 us
    psum x1, blocking collectives, local(): lax.psum(jnp.sum(value_error[:, None] * attn_flat, 0), ('outer', 'inner'))  95.9 us
    dot_general x2, matrix products, logits_of(): jnp.einsum('qhgd,khd->hgqk', query_heads, key_rows.reshape(-1, heads_kv,...  91.9 us
    dot_general x1, matrix products, block_grads(): jnp.einsum('qhgd,khd->hgqk', dout_heads, value_heads, preferred_element_t...  79.6 us
    all_gather x1, waiting for transfers between devices, local(): lax.all_gather(keys, ('outer', 'inner'), axis=0, tiled=True)  62.7 us
    dot_general x1, matrix products, compute(): jnp.einsum('hgqk,khd->qhgd', attn_prob.astype(jnp.bfloat16), value_heads,...  51.9 us
    dot_general x1, matrix products, block_grads(): jnp.einsum('hgqk,qhgd->khd', prob_low, dout_heads, preferred_element_type...  46.7 us
  transfers between devices with their start and end apart: 3, of which 2 were waited for; matrix products, arithmetic and copies ran while one was open for 1% of the time, Pallas kernels for 0%

commit v1 on v0

v1 whole, which is shorter than its diff:
```python
import functools
import math

import jax
import jax.numpy as jnp
from jax import lax
from jax.experimental import pallas as pl
from jax.experimental.pallas import tpu as pltpu
from jax.sharding import PartitionSpec as P

HD = 128
BLK = 256
NB = 32
HPD = 4
WIDTH = HPD * HD
PAD = 16
SCALE = HD ** (-0.5)
SCALE2 = SCALE * math.log2(math.e)
NEG = -1e30
CTX = ("outer", "inner")
NT = (((1,), (1,)), ((), ()))
F32 = jnp.float32
BF16 = jnp.bfloat16
VMEM_LIMIT = 52 * 1024 * 1024


def dot(a, b):
    return jnp.dot(a, b, preferred_element_type=F32)


def dot_nt(a, b):
    return lax.dot_general(a, b, NT, preferred_element_type=F32)


def rows(b):
    return pl.ds(pl.multiple_of(b * BLK, BLK), BLK)


def block_of(scal, o, dz, dy):
    z = (scal[12] + dz) & 3
    y = (scal[13] + dy) & 3
    return 16 * o + 4 * z + y


def place_keys(scal, kp, put):
    for dy in range(4):
        for dz in range(4):
            for o in range(2):
                put(block_of(scal, o, dz, dy), kp[dy][dz, o, :BLK, :])


def place_values(scal, vp, put):
    for dz in range(4):
        for dy in range(4):
            for o in range(2):
                put(block_of(scal, o, dz, dy), vp[dz][dy, o])


def start_of(scal, pos):
    lo = jnp.zeros_like(pos)
    for v in range(1, 8):
        lo = jnp.maximum(lo, jnp.where(pos >= scal[v], scal[v], 0))
    return lo


def allowed_of(scal, base, kb):
    query_pos = base + lax.broadcasted_iota(jnp.int32, (1, BLK), 1)
    lo = start_of(scal, query_pos)
    key_pos = kb * BLK + lax.broadcasted_iota(jnp.int32, (BLK, BLK), 0)
    return (key_pos <= query_pos) & (key_pos >= lo)


def sweep(scal, base, body):
    diag = base // BLK
    first = start_of(scal, base) // BLK
    full = (start_of(scal, base + BLK - 1) + BLK - 1) // BLK
    full = jnp.minimum(full, diag)

    def masked(t, c):
        kb = jnp.where(t == 0, diag, first + t - 1)
        body(kb, True)
        return c

    def plain(kb, c):
        body(kb, False)
        return c

    lax.fori_loop(0, full - first + 1, masked, 0)
    lax.fori_loop(full, diag, plain, 0)


def forward_kernel(
    scal, q0, q1, q2, q3, k0, k1, k2, k3, v0, v1, v2, v3, w_ref,
    out_ref, lse_ref, critic_ref,
    q_all, k_all, vt_all, acc, top, tot,
):
    for p, q in enumerate((q0, q1, q2, q3)):
        q_all[p] = q[...]

    def put_k(b, blk):
        k_all[rows(b), :] = blk

    def put_v(b, blk):
        vt_all[b] = blk.T

    place_keys(scal, (k0, k1, k2, k3), put_k)
    place_values(scal, (v0, v1, v2, v3), put_v)

    def piece(p, c):
        base = scal[8 + p]
        top[...] = jnp.full_like(top, NEG)
        tot[...] = jnp.zeros_like(tot)
        acc[...] = jnp.zeros_like(acc)

        def body(kb, masked):
            k_blk = k_all[rows(kb), :]
            vt_blk = vt_all[kb]
            if masked:
                allowed = allowed_of(scal, base, kb)
            for h in range(HPD):
                s = dot_nt(k_blk, q_all[p, :, h * HD:(h + 1) * HD])
                if masked:
                    s = jnp.where(allowed, s, NEG)
                old = top[h]
                new = jnp.maximum(old, jnp.max(s, 0, keepdims=True))
                prob = jnp.exp2(s * SCALE2 - new * SCALE2)
                fade = jnp.exp2((old - new) * SCALE2)
                top[h] = new
                tot[h] = tot[h] * fade + jnp.sum(prob, 0, keepdims=True)
                acc[h] = acc[h] * fade + dot(vt_blk, prob.astype(BF16))

        sweep(scal, base, body)
        critic = jnp.zeros((1, BLK), F32)
        for h in range(HPD):
            total = tot[h]
            out = (acc[h] / total).astype(BF16)
            out_ref[p, h] = out
            lse_ref[p, h] = top[h] * SCALE2 + jnp.log2(total)
            w = w_ref[h * HD:(h + 1) * HD, :]
            critic += jnp.sum(out.astype(F32) * jnp.concatenate([w, w], 1), 0, keepdims=True)
        critic_ref[p] = critic
        return c

    lax.fori_loop(0, 4, piece, 0)


def backward_kernel(
    scal, q0, q1, q2, q3, u0, u1, u2, u3, k0, k1, k2, k3, v0, v1, v2, v3,
    w_ref, out_ref, lse_ref, err_ref,
    dq_ref, dk0, dk1, dk2, dk3, dv0, dv1, dv2, dv3, readout_ref,
    q_all, k_all, kt_all, v_all, do_all, dot_all, delta_all, dk_all, dv_all, dqt,
):
    for p, q in enumerate((q0, q1, q2, q3)):
        q_all[p] = q[...]

    def put_k(b, blk):
        k_all[rows(b), :] = blk
        kt_all[b] = blk.T

    def put_v(b, blk):
        v_all[rows(b), :] = blk

    place_keys(scal, (k0, k1, k2, k3), put_k)
    place_values(scal, (v0, v1, v2, v3), put_v)
    dk_all[...] = jnp.zeros_like(dk_all)
    dv_all[...] = jnp.zeros_like(dv_all)
    for h in range(HPD):
        cols = slice(h * HD, (h + 1) * HD)
        w = w_ref[cols, :]
        w = jnp.concatenate([w, w], 1)
        readout = jnp.zeros((HD, BLK), F32)
        for p, u in enumerate((u0, u1, u2, u3)):
            err = err_ref[p]
            out = out_ref[p, h].astype(F32)
            dout = (err * w + u[:, cols].T.astype(F32)).astype(BF16)
            dot_all[p, h] = dout
            do_all[p, h] = dout.T
            delta_all[p, h] = jnp.sum(dout.astype(F32) * out, 0, keepdims=True)
            readout += err * out
        readout_ref[cols, :] = jnp.sum(readout, 1, keepdims=True)

    def piece(p, c):
        base = scal[8 + p]
        dqt[...] = jnp.zeros_like(dqt)

        def body(kb, masked):
            k_blk = k_all[rows(kb), :]
            v_blk = v_all[rows(kb), :]
            kt_blk = kt_all[kb]
            if masked:
                allowed = allowed_of(scal, base, kb)
            dk = jnp.zeros((BLK, HD), F32)
            dv = jnp.zeros((BLK, HD), F32)
            for h in range(HPD):
                q = q_all[p, :, h * HD:(h + 1) * HD]
                prob = jnp.exp2(dot_nt(k_blk, q) * SCALE2 - lse_ref[p, h])
                if masked:
                    prob = jnp.where(allowed, prob, 0.0)
                dprob = dot(v_blk, dot_all[p, h])
                dlogit = (prob * (dprob - delta_all[p, h])).astype(BF16)
                dv += dot(prob.astype(BF16), do_all[p, h])
                dk += dot(dlogit, q)
                dqt[h] += dot(kt_blk, dlogit)
            dk_all[rows(kb), :] += dk
            dv_all[rows(kb), :] += dv

        sweep(scal, base, body)
        for h in range(HPD):
            dq_ref[p, :, h * HD:(h + 1) * HD] = (dqt[h] * SCALE).T.astype(BF16)
        return c

    lax.fori_loop(0, 4, piece, 0)

    for dy, dk in enumerate((dk0, dk1, dk2, dk3)):
        for dz in range(4):
            for o in range(2):
                b = block_of(scal, o, dz, dy)
                dk[dz, o] = (dk_all[rows(b), :] * SCALE).astype(BF16)
    for dz, dv in enumerate((dv0, dv1, dv2, dv3)):
        for dy in range(4):
            for o in range(2):
                b = block_of(scal, o, dz, dy)
                dv[dy, o] = dv_all[rows(b), :].astype(BF16)


SMEM_SPEC = pl.BlockSpec(memory_space=pltpu.SMEM)
VMEM_SPEC = pl.BlockSpec(memory_space=pltpu.VMEM)


def forward(scal, qs, kp, vp, w):
    return pl.pallas_call(
        forward_kernel,
        out_shape=(
            jax.ShapeDtypeStruct((4, HPD, HD, BLK), BF16),
            jax.ShapeDtypeStruct((4, HPD, 1, BLK), F32),
            jax.ShapeDtypeStruct((4, 1, BLK), F32),
        ),
        in_specs=[SMEM_SPEC] + [VMEM_SPEC] * 13,
        out_specs=(VMEM_SPEC,) * 3,
        scratch_shapes=[
            pltpu.VMEM((4, BLK, WIDTH), BF16),
            pltpu.VMEM((NB * BLK, HD), BF16),
            pltpu.VMEM((NB, HD, BLK), BF16),
            pltpu.VMEM((HPD, HD, BLK), F32),
            pltpu.VMEM((HPD, 1, BLK), F32),
            pltpu.VMEM((HPD, 1, BLK), F32),
        ],
        compiler_params=pltpu.CompilerParams(vmem_limit_bytes=VMEM_LIMIT),
        cost_estimate=pl.CostEstimate(flops=9 * 10**9, bytes_accessed=8 << 20, transcendentals=10**7),
        name="attention_forward",
    )(scal, *qs, *kp, *vp, w)


def backward(scal, qs, us, kp, vp, w, out, lse, err):
    piece = jax.ShapeDtypeStruct((4, 2, BLK, HD), BF16)
    return pl.pallas_call(
        backward_kernel,
        out_shape=(
            jax.ShapeDtypeStruct((4, BLK, WIDTH), BF16),
            *([piece] * 8),
            jax.ShapeDtypeStruct((WIDTH, 1), F32),
        ),
        in_specs=[SMEM_SPEC] + [VMEM_SPEC] * 20,
        out_specs=(VMEM_SPEC,) * 10,
        scratch_shapes=[
            pltpu.VMEM((4, BLK, WIDTH), BF16),
            pltpu.VMEM((NB * BLK, HD), BF16),
            pltpu.VMEM((NB, HD, BLK), BF16),
            pltpu.VMEM((NB * BLK, HD), BF16),
            pltpu.VMEM((4, HPD, BLK, HD), BF16),
            pltpu.VMEM((4, HPD, HD, BLK), BF16),
            pltpu.VMEM((4, HPD, 1, BLK), F32),
            pltpu.VMEM((NB * BLK, HD), F32),
            pltpu.VMEM((NB * BLK, HD), F32),
            pltpu.VMEM((HPD, HD, BLK), F32),
        ],
        compiler_params=pltpu.CompilerParams(vmem_limit_bytes=VMEM_LIMIT),
        cost_estimate=pl.CostEstimate(flops=25 * 10**9, bytes_accessed=16 << 20, transcendentals=10**7),
        name="attention_backward",
    )(scal, *qs, *us, *kp, *vp, w, out, lse, err)


def send(x, move):
    pairs = []
    for b in range(NB):
        o, z, y = move(b // 16, b // 4 % 4, b % 4)
        pairs.append((b, 16 * o + 4 * (z % 4) + y % 4))
    return lax.ppermute(x, CTX, pairs)


def swap(x, k):
    def move(o, z, y):
        if k & 1:
            z, y = 3 - z, 3 - y
        return (o ^ (k >> 1), z, y)

    return send(x, move)


def from_z(x, d):
    return send(x, lambda o, z, y: (o, z - d, y))


def from_y(x, d):
    return send(x, lambda o, z, y: (o, z, y - d))


def quarter(x, index):
    return lax.dynamic_slice_in_dim(x, index * WIDTH, WIDTH, 1)


def total_of(parts):
    return functools.reduce(jnp.add, [x.astype(F32) for x in parts])


def local(queries, keys, values, segment_ids, value_weight, targets, upstream):
    o = lax.axis_index("outer")
    i = lax.axis_index("inner")
    head = lax.axis_index("head")
    z, y = i // 4, i % 4
    member = 2 * o + i // 8

    below = jnp.sum(
        segment_ids[:, None] < jnp.arange(HD, dtype=jnp.int32)[None, :], 0, dtype=jnp.int32
    )
    below = jnp.where(jnp.arange(HD) < 8, below, 0).astype(F32).astype(BF16)
    pad = jnp.concatenate([below[None, :], jnp.zeros((PAD - 1, HD), BF16)], 0)

    def packed(index):
        k = lax.dynamic_slice_in_dim(keys, index * HD, HD, 1)
        v = lax.dynamic_slice_in_dim(values, index * HD, HD, 1)
        return jnp.concatenate([k, pad, v], 0)

    mine = packed(o)
    other = swap(packed(1 - o), 2)
    pair = jnp.stack([jnp.where(o == 0, mine, other), jnp.where(o == 0, other, mine)])
    k_pair, v_pair = pair[:, : BLK + PAD], pair[:, BLK + PAD:]
    k_line = jnp.stack([k_pair] + [from_z(k_pair, d) for d in (1, 2, 3)])
    v_line = jnp.stack([v_pair] + [from_y(v_pair, d) for d in (1, 2, 3)])
    kp = [k_line] + [from_y(k_line, d) for d in (1, 2, 3)]
    vp = [v_line] + [from_z(v_line, d) for d in (1, 2, 3)]
    starts = jnp.sum(total_of([k[:, :, BLK, :8] for k in kp]), (0, 1)).astype(jnp.int32)

    qs = [quarter(queries, member)] + [swap(quarter(queries, member ^ k), k) for k in (1, 2, 3)]
    us = [quarter(upstream, member)] + [swap(quarter(upstream, member ^ k), k) for k in (1, 2, 3)]
    bases = [
        BLK * (16 * (o ^ (k >> 1)) + (15 - i if k & 1 else i)) for k in range(4)
    ]
    scal = jnp.concatenate(
        [starts, jnp.stack(bases + [z, y, z, y]).astype(jnp.int32)]
    )
    w = jnp.broadcast_to(
        lax.dynamic_slice_in_dim(value_weight, member * WIDTH, WIDTH, 0)[:, None], (WIDTH, HD)
    )

    out, lse, critic = forward(scal, qs, kp, vp, w)

    critic = critic[:, 0, :]
    critic = critic - jnp.concatenate(
        [jnp.where(head == 0, targets, 0.0)[None, :], jnp.zeros((3, BLK), F32)], 0
    )
    critic = lax.psum(critic, "head")
    err = critic
    for k in (1, 2, 3):
        got = swap(critic, k)
        err = err + jnp.stack([got[p ^ k] for p in range(4)])
    value_error = err[0]

    dq, *grads, readout = backward(scal, qs, us, kp, vp, w, out, lse, err[:, None, :])
    dk, dv = grads[:4], grads[4:]

    got = [dq[0]] + [swap(dq[k], k) for k in (1, 2, 3)]
    query_grad = jnp.concatenate(
        [
            jnp.select([member == m for m in range(3)], [got[c ^ m] for m in range(3)], got[c ^ 3])
            for c in range(4)
        ],
        1,
    )

    dk_line = total_of([dk[0]] + [send(dk[d], lambda o, z, y, d=d: (o, z, y + d)) for d in (1, 2, 3)])
    dv_line = total_of([dv[0]] + [send(dv[d], lambda o, z, y, d=d: (o, z + d, y)) for d in (1, 2, 3)])
    dk_line, dv_line = dk_line.astype(BF16), dv_line.astype(BF16)
    dk_pair = total_of(
        [dk_line[0]] + [send(dk_line[d], lambda o, z, y, d=d: (o, z + d, y)) for d in (1, 2, 3)]
    )
    dv_pair = total_of(
        [dv_line[0]] + [send(dv_line[d], lambda o, z, y, d=d: (o, z, y + d)) for d in (1, 2, 3)]
    )
    pair = jnp.concatenate([dk_pair, dv_pair], 2).astype(BF16)
    mine = jnp.where(o == 0, pair[0], pair[1])
    other = swap(jnp.where(o == 0, pair[1], pair[0]), 2)
    low, high = jnp.where(o == 0, mine, other), jnp.where(o == 0, other, mine)
    key_grad = jnp.concatenate([low[:, :HD], high[:, :HD]], 1)
    value_grad = jnp.concatenate([low[:, HD:], high[:, HD:]], 1)

    spread = lax.dynamic_update_slice_in_dim(
        jnp.zeros((4, WIDTH), F32), readout[:, 0][None, :], member, 0
    )
    line = total_of([spread] + [from_y(spread, d) for d in (1, 2, 3)])
    line = total_of([line] + [from_z(line, d) for d in (1, 2, 3)])
    readout_grad = (line + swap(line, 2)).reshape(-1)
    return (query_grad, key_grad, value_grad, value_error, readout_grad)


def solution(mesh):
    return jax.shard_map(
        local,
        mesh=mesh,
        in_specs=(
            P(CTX, "head"),
            P(CTX, "head"),
            P(CTX, "head"),
            P(CTX),
            P("head"),
            P(CTX),
            P(CTX, "head"),
        ),
        out_specs=(
            P(CTX, "head"),
            P(CTX, "head"),
            P(CTX, "head"),
            P(CTX),
            P("head"),
        ),
        check_vma=False,
    )
```

time: 817 us -> 337 us (0.41)
  matrix products: 325 us -> 0 us
  blocking collectives: 199 us -> 5.67 us
  Pallas kernels: 0 us -> 114 us
  starting transfers between devices: 0.12 us -> 83.2 us
  other arithmetic: 66.9 us -> 7.29 us
  waiting for transfers between devices: 169 us -> 114 us
  local copies, waits for them, and re-layouts: 40.3 us -> 5.57 us
  between operations: 15.1 us -> 2.98 us
    dot_general x7 -> x0, matrix products: 325 us -> none  [the longest x2 91.9 us: logits_of(): jnp.einsum('qhgd,khd->hgqk', query_heads, key_rows.reshape(-1, heads_kv,...]
    pallas_call x0 -> x2, Pallas kernels: none -> 114 us  [the longest x1 59.2 us: forward(): pl.pallas_call(forward_kernel, out_shape=(jax.ShapeDtypeStruct((4, HPD, H...]
    ppermute x0 -> x45, waiting for transfers between devices: none -> 114 us  [send(): return lax.ppermute(x, CTX, pairs)]
    reduce_scatter x1 -> x0, waiting for transfers between devices: 106 us -> none  [local(): lax.psum_scatter(buffer.astype(jnp.bfloat16), ('outer', 'inner'), scatter...]
    all_gather x1 -> x0, blocking collectives: 96.7 us -> none  [local(): lax.all_gather(segment_ids, ('outer', 'inner'), axis=0, tiled=True)]
    psum x2 -> x1, blocking collectives: 102 us -> 5.67 us  [local(): critic = lax.psum(critic, 'head')]
    ppermute x0 -> x45, starting transfers between devices: none -> 83.2 us  [send(): return lax.ppermute(x, CTX, pairs)]
    all_gather x2 -> x0, waiting for transfers between devices: 62.7 us -> none  [the longest x1 62.7 us: local(): lax.all_gather(keys, ('outer', 'inner'), axis=0, tiled=True)]
  transfers between devices with their start and end apart: 3 -> 45, of which waited for: 2 -> 20; matrix products, arithmetic and copies ran while one was open for 1% -> 2% of each run, Pallas kernels for 0% -> 0%
where the time goes in v1:
time: 337 us; the launch traced here: 333 us
  waiting for transfers between devices  114 us (34%)
  Pallas kernels  114 us (34%)
  starting transfers between devices  83.2 us (25%)
  other arithmetic  7.29 us (2%)
  blocking collectives  5.67 us (2%)
  local copies, waits for them, and re-layouts  5.57 us (2%)
    ppermute x45, waiting for transfers between devices, send(): return lax.ppermute(x, CTX, pairs)  114 us
    ppermute x45, starting transfers between devices, send(): return lax.ppermute(x, CTX, pairs)  83.2 us
    pallas_call x1, Pallas kernels, forward(): pl.pallas_call(forward_kernel, out_shape=(jax.ShapeDtypeStruct((4, HPD, H...  59.2 us
    pallas_call x1, Pallas kernels, backward(): pl.pallas_call(backward_kernel, out_shape=(jax.ShapeDtypeStruct((4, BLK,...  55.2 us
  transfers between devices with their start and end apart: 45, of which 20 were waited for; matrix products, arithmetic and copies ran while one was open for 2% of the time, Pallas kernels for 0%

profile of v1, /device:TPU:0, one launch (start us, length us, event | category | flops | bytes accessed | tf_op | source)
XLA Modules:
  0.0 332.7 jit_solution(8508567980098533426)
XLA Ops:
  0.6 0.8 convert_reduce_fusion
  1.5 1.0 constant_dynamic-slice_fusion.11
  2.6 3.2 collective-permute-start
  5.8 3.6 %collective-permute-done = bf16[528,128]{1,0:T(8,128)(2,1)S(1)} collective-permute-done((bf16[528,128]{1,0:T(8,128)(2,1)S(1)}, bf16[528,128]{1,0:T(8,128)(2,1)S(1)}, u32[]{:S(2)}, u32[]{:S(2)}) %collective-permute-start) | collective-permute-done | bytes 135200 | tf_op jit(solution)/shard_map/ppermute | solution.py:288
  9.6 4.3 %collective-permute-start.1 = (bf16[2,272,128]{2,1,0:T(8,128)(2,1)S(1)}, bf16[2,272,128]{2,1,0:T(8,128)(2,1)S(1)}, u32[]{:S(2)}, u32[]{:S(2)}) collective-permute-start(bf16[2,272,128]{2,1,0:T(8,128)(2,1)S(1)} %fusion.10), channel_id=1, source_target_pairs={{0,12},{1,13},{2,14},{3,15},{4,0},{5,1},{6,2},{7,3},{8,4},{9,5},{1... | collective-permute-start | bytes 417800 | tf_op jit(solution)/shard_map/ppermute | solution.py:288
  13.9 1.3 collective-permute-start.3
  15.2 3.8 %collective-permute-done.1 = bf16[2,272,128]{2,1,0:T(8,128)(2,1)S(1)} collective-permute-done((bf16[2,272,128]{2,1,0:T(8,128)(2,1)S(1)}, bf16[2,272,128]{2,1,0:T(8,128)(2,1)S(1)}, u32[]{:S(2)}, u32[]{:S(2)}) %collective-permute-start.1) | collective-permute-done | bytes 139296 | tf_op jit(solution)/shard_map/ppermute | solution.py:288
  18.9 2.3 collective-permute-done.2
  21.3 1.1 collective-permute-done.3
  22.5 3.1 collective-permute-start.4
  25.5 0.8 collective-permute-start.13
  26.7 3.2 collective-permute-start.5
  29.9 1.3 collective-permute-start.6
  31.3 24.5 %collective-permute-done.13 = bf16[2,256,128]{2,1,0:T(8,128)(2,1)S(1)} collective-permute-done((bf16[2,256,128]{2,1,0:T(8,128)(2,1)S(1)}, bf16[2,256,128]{2,1,0:T(8,128)(2,1)S(1)}, u32[]{:S(2)}, u32[]{:S(2)}) %collective-permute-start.13) | collective-permute-done | bytes 131104 | tf_op jit(solution)/shard_map/ppermute | solution.py:288
  55.8 3.2 collective-permute-start.7
  59.0 6.2 %collective-permute-done.15 = bf16[2,256,128]{2,1,0:T(8,128)(2,1)S(1)} collective-permute-done((bf16[2,256,128]{2,1,0:T(8,128)(2,1)S(1)}, bf16[2,256,128]{2,1,0:T(8,128)(2,1)S(1)}, u32[]{:S(2)}, u32[]{:S(2)}) %collective-permute-start.15) | collective-permute-done | bytes 131104 | tf_op jit(solution)/shard_map/ppermute | solution.py:288
  65.3 3.2 collective-permute-start.16
  68.5 1.0 collective-permute-start.18
  69.4 0.8 dynamic_slice.51
  70.2 3.0 collective-permute-start.8
  73.2 4.5 %collective-permute-start.9 = (bf16[256,512]{1,0:T(8,128)(2,1)S(1)}, bf16[256,512]{1,0:T(8,128)(2,1)S(1)}, u32[]{:S(2)}, u32[]{:S(2)}) collective-permute-start(bf16[256,512]{1,0:T(8,128)(2,1)S(1)} %get-tuple-element.44), channel_id=1, source_target_pairs={{0,31},{1,30},{2,29},{3,28},{4,27},{5,26},{6,25},{7,24},{8,23},{9,... | collective-permute-start | bytes 786440 | tf_op jit(solution)/shard_map/ppermute | solution.py:288
  77.8 0.8 fusion.21
  78.6 6.9 %collective-permute-done.9.q3 = bf16[256,512]{1,0:T(8,128)(2,1)S(1)} collective-permute-done((bf16[256,512]{1,0:T(8,128)(2,1)S(1)}, bf16[256,512]{1,0:T(8,128)(2,1)S(1)}, u32[]{:S(2)}, u32[]{:S(2)}) %collective-permute-start.9) | collective-permute-done | bytes 262176 | tf_op jit(solution)/shard_map/ppermute | solution.py:288
  85.6 5.3 %collective-permute-done.16.v1 = bf16[4,2,256,128]{3,2,1,0:T(8,128)(2,1)} collective-permute-done((bf16[4,2,256,128]{3,2,1,0:T(8,128)(2,1)S(1)}, bf16[4,2,256,128]{3,2,1,0:T(8,128)(2,1)}, u32[]{:S(2)}, u32[]{:S(2)}) %collective-permute-start.16) | collective-permute-done | bytes 524320 | tf_op jit(solution)/shard_map/ppermute | solution.py:288
  90.9 2.8 collective-permute-done.18.v3
  93.8 59.2 %attention_forward.1 = (bf16[4,4,128,256]{3,2,1,0:T(8,128)(2,1)}, f32[4,4,1,256]{3,2,1,0:T(1,128)S(1)}, f32[4,1,256]{2,1,0:T(1,128)S(1)}) custom-call(s32[16]{0:T(128)S(1)} %concatenate.30.scal, bf16[256,512]{1,0:T(8,128)(2,1)S(1)} %get-tuple-element.46.q0, bf16[256,512]{1,0:T(8,128)(2,1)S(1)} %collective-permute-done.7.q1, ...), custom_call_target="tpu_custom_call" | custom-call | flops 8999999488 | bytes 8388608 | tf_op jit(solution)/shard_map/attention_forward/pallas_call | solution.py:231
  153.1 5.7 %psum.7 = f32[4,256]{1,0:T(4,128)S(1)} all-reduce(f32[4,256]{1,0:T(4,128)S(1)} %bitcast_subtract_fusion), channel_id=1, replica_groups=mesh['head'=4,'outer'=2,'inner'=16] {'head'}, use_global_device_ids=true, to_apply=%region_3.4 | all-reduce | flops 1024 | bytes 8192 | tf_op jit(solution)/shard_map/psum | solution.py:362
  158.7 3.3 collective-permute-start.21
  162.1 4.8 %collective-permute-start.10 = (bf16[256,512]{1,0:T(8,128)(2,1)S(1)}, bf16[256,512]{1,0:T(8,128)(2,1)S(1)}, u32[]{:S(2)}, u32[]{:S(2)}) collective-permute-start(bf16[256,512]{1,0:T(8,128)(2,1)S(1)} %get-tuple-element.41), channel_id=1, source_target_pairs={{0,15},{1,14},{2,13},{3,12},{4,11},{5,10},{6,9},{7,8},{8,7},{9,6},... | collective-permute-start | bytes 786440 | tf_op jit(solution)/shard_map/ppermute | solution.py:288
  167.3 3.2 collective-permute-start.12
  171.0 4.6 %collective-permute-start.19 = (f32[4,256]{1,0:T(4,128)S(1)}, f32[4,256]{1,0:T(4,128)S(1)}, u32[]{:S(2)}, u32[]{:S(2)}) collective-permute-start(f32[4,256]{1,0:T(4,128)S(1)} %psum.7), channel_id=1, source_target_pairs={{0,15},{1,14},{2,13},{3,12},{4,11},{5,10},{6,9},{7,8},{8,7},{9,6},... | collective-permute-start | bytes 12296 | tf_op jit(solution)/shard_map/ppermute | solution.py:288
  175.6 5.9 %collective-permute-done.20 = f32[4,256]{1,0:T(4,128)S(1)} collective-permute-done((f32[4,256]{1,0:T(4,128)S(1)}, f32[4,256]{1,0:T(4,128)S(1)}, u32[]{:S(2)}, u32[]{:S(2)}) %collective-permute-start.20) | collective-permute-done | bytes 4128 | tf_op jit(solution)/shard_map/ppermute | solution.py:288
  181.6 0.7 copy-done.10
  182.4 55.2 %attention_backward.1 = (bf16[4,256,512]{2,1,0:T(8,128)(2,1)}, bf16[4,2,256,128]{3,2,1,0:T(8,128)(2,1)}, bf16[4,2,256,128]{3,2,1,0:T(8,128)(2,1)}, bf16[4,2,256,...) custom-call(s32[16]{0:T(128)S(1)} %concatenate.30.scal, ...), custom_call_target="tpu_custom_call" | custom-call | flops 24999999488 | bytes 16777216 | tf_op jit(solution)/shard_map/attention_backward/pallas_call | solution.py:256
  237.9 3.8 %collective-permute-start.39 = (f32[4,512]{1,0:T(4,128)S(1)}, f32[4,512]{1,0:T(4,128)S(1)}, u32[]{:S(2)}, u32[]{:S(2)}) collective-permute-start(f32[4,512]{1,0:T(4,128)S(1)} %dynamic_update_slice.5), channel_id=1, source_target_pairs={{0,2},{1,3},{2,0},{3,1},{4,6},{5,7},{6,4},{7,5},{8,10},{9,11},{10,... | collective-permute-start | bytes 24584 | tf_op jit(solution)/shard_map/ppermute | solution.py:288
  241.7 0.8 collective-permute-start.40
  242.5 1.2 slice_bitcast_fusion.1
  243.7 5.4 %collective-permute-start.22 = (bf16[256,512]{1,0:T(8,128)(2,1)S(1)}, bf16[256,512]{1,0:T(8,128)(2,1)S(1)}, u32[]{:S(2)}, u32[]{:S(2)}) collective-permute-start(bf16[256,512]{1,0:T(8,128)(2,1)S(1)} %get-tuple-element.39), channel_id=1, source_target_pairs={{0,31},{1,30},{2,29},{3,28},{4,27},{5,26},{6,25},{7,24},{8,23},{9,... | collective-permute-start | bytes 786440 | tf_op jit(solution)/shard_map/ppermute | solution.py:288
  249.2 1.5 collective-permute-start.41
  250.7 0.9 collective-permute-start.43
  251.6 1.3 collective-permute-done.41
  252.9 3.0 collective-permute-done.42
  256.1 2.3 collective-permute-start.44
  258.4 2.1 collective-permute-start.26
  260.4 1.2 collective-permute-start.27
  261.6 2.3 collective-permute-start.23
  263.9 1.1 collective-permute-start.24
  265.0 0.7 add_reduce_fusion
  268.8 17.4 %collective-permute-done.23 = bf16[256,512]{1,0:T(8,128)(2,1)S(1)} collective-permute-done((bf16[256,512]{1,0:T(8,128)(2,1)S(1)}, bf16[256,512]{1,0:T(8,128)(2,1)S(1)}, u32[]{:S(2)}, u32[]{:S(2)}) %collective-permute-start.23) | collective-permute-done | bytes 262176 | tf_op jit(solution)/shard_map/ppermute | solution.py:288
  286.3 3.0 collective-permute-start.32
  289.3 1.1 fusion.6
  290.4 1.0 collective-permute-start.33
  291.7 1.2 collective-permute-start.28
  292.9 1.5 collective-permute-start.29
  294.4 18.8 %collective-permute-done.31 = bf16[4,2,256,128]{3,2,1,0:T(8,128)(2,1)S(1)} collective-permute-done((bf16[4,2,256,128]{3,2,1,0:T(8,128)(2,1)}, bf16[4,2,256,128]{3,2,1,0:T(8,128)(2,1)S(1)}, u32[]{:S(2)}, u32[]{:S(2)}) %collective-permute-start.31) | collective-permute-done | bytes 524320 | tf_op jit(solution)/shard_map/ppermute | solution.py:288
  314.0 1.8 collective-permute-start.34
  315.8 3.8 %collective-permute-start.35 = (bf16[2,256,128]{2,1,0:T(8,128)(2,1)S(1)}, bf16[2,256,128]{2,1,0:T(8,128)(2,1)S(1)}, u32[]{:S(2)}, u32[]{:S(2)}) collective-permute-start(bf16[2,256,128]{2,1,0:T(8,128)(2,1)S(1)} %get-tuple-element.53), channel_id=1, source_target_pairs={{0,2},{1,3},{2,0},{3,1},{4,6},{5,7},{6,4},{7,5},{8,10},{9,11},{10,... | collective-permute-start | bytes 393224 | tf_op jit(solution)/shard_map/ppermute | solution.py:288
  319.7 2.6 collective-permute-done.34
  322.3 1.7 collective-permute-done.35
  324.0 0.6 collective-permute-done.36
  325.2 1.1 pad_maximum_fusion
  326.3 5.0 %collective-permute-done.37 = bf16[256,256]{1,0:T(8,128)(2,1)S(1)} collective-permute-done((bf16[256,256]{1,0:T(8,128)(2,1)S(1)}, bf16[256,256]{1,0:T(8,128)(2,1)S(1)}, u32[]{:S(2)}, u32[]{:S(2)}) %collective-permute-start.37) | collective-permute-done | bytes 131104 | tf_op jit(solution)/shard_map/ppermute | solution.py:288
  331.4 0.7 pad_maximum_fusion.8
  332.1 0.7 pad_maximum_fusion.7
  (106 shorter events, 6.1 us)
Async XLA Ops:
  2.6 6.8 %collective-permute-start = (bf16[528,128]{1,0:T(8,128)(2,1)S(1)}, bf16[528,128]{1,0:T(8,128)(2,1)S(1)}, u32[]{:S(2)}, u32[]{:S(2)}) collective-permute-start(bf16[528,128]{1,0:T(8,128)(2,1)S(1)} %fusion.14), channel_id=1, source_target_pairs={{0,16},{1,17},{2,18},{3,19},{4,20},{5,21},{6,22},{7,23},{8,24},{9,... | collective-permute-start | bytes 405512 | tf_op jit(solution)/shard_map/ppermute | solution.py:288
  9.6 21.6 %copy-start.2 = (bf16[256,2048]{1,0:T(8,128)(2,1)S(1)}, bf16[256,2048]{1,0:T(8,128)(2,1)}, u32[]{:S(2)}) copy-start(bf16[256,2048]{1,0:T(8,128)(2,1)} %param.7) | copy-start | bytes 3145732
  9.6 9.4 %collective-permute-start.1 = (bf16[2,272,128]{2,1,0:T(8,128)(2,1)S(1)}, bf16[2,272,128]{2,1,0:T(8,128)(2,1)S(1)}, u32[]{:S(2)}, u32[]{:S(2)}) collective-permute-start(bf16[2,272,128]{2,1,0:T(8,128)(2,1)S(1)} %fusion.10), channel_id=1, source_target_pairs={{0,12},{1,13},{2,14},{3,15},{4,0},{5,1},{6,2},{7,3},{8,4},{9,5},{1... | collective-permute-start | bytes 417800 | tf_op jit(solution)/shard_map/ppermute | solution.py:288
  13.9 7.4 %collective-permute-start.2 = (bf16[2,272,128]{2,1,0:T(8,128)(2,1)S(1)}, bf16[2,272,128]{2,1,0:T(8,128)(2,1)S(1)}, u32[]{:S(2)}, u32[]{:S(2)}) collective-permute-start(bf16[2,272,128]{2,1,0:T(8,128)(2,1)S(1)} %fusion.10), channel_id=1, source_target_pairs={{0,8},{1,9},{2,10},{3,11},{4,12},{5,13},{6,14},{7,15},{8,0},{9,1},... | collective-permute-start | bytes 417800 | tf_op jit(solution)/shard_map/ppermute | solution.py:288
  13.9 8.5 %collective-permute-start.3 = (bf16[2,272,128]{2,1,0:T(8,128)(2,1)S(1)}, bf16[2,272,128]{2,1,0:T(8,128)(2,1)S(1)}, u32[]{:S(2)}, u32[]{:S(2)}) collective-permute-start(bf16[2,272,128]{2,1,0:T(8,128)(2,1)S(1)} %fusion.10), channel_id=1, source_target_pairs={{0,4},{1,5},{2,6},{3,7},{4,8},{5,9},{6,10},{7,11},{8,12},{9,13},{1... | collective-permute-start | bytes 417800 | tf_op jit(solution)/shard_map/ppermute | solution.py:288
  22.4 55.3 %copy-start.4 = (bf16[4,2,272,128]{3,2,1,0:T(8,128)(2,1)}, bf16[4,2,272,128]{3,2,1,0:T(8,128)(2,1)S(1)}, u32[]{:S(2)}) copy-start(bf16[4,2,272,128]{3,2,1,0:T(8,128)(2,1)S(1)} %pad_maximum_fusion.1.k0) | copy-start | bytes 1671172
  22.5 46.0 %collective-permute-start.4 = (bf16[4,2,272,128]{3,2,1,0:T(8,128)(2,1)S(1)}, bf16[4,2,272,128]{3,2,1,0:T(8,128)(2,1)}, u32[]{:S(2)}, u32[]{:S(2)}) collective-permute-start(bf16[4,2,272,128]{3,2,1,0:T(8,128)(2,1)S(1)} %pad_maximum_fusion.1.k0), channel_id=1, source_target_pairs={{0,3},{1,0},{2,1},{3,2},{4,7},{5,4},{6,5},{7,6},{8,11},{9,8},{10,9... | collective-permute-start | bytes 1671176 | tf_op jit(solution)/shard_map/ppermute | solution.py:288
  25.5 30.2 %collective-permute-start.13 = (bf16[2,256,128]{2,1,0:T(8,128)(2,1)S(1)}, bf16[2,256,128]{2,1,0:T(8,128)(2,1)S(1)}, u32[]{:S(2)}, u32[]{:S(2)}) collective-permute-start(bf16[2,256,128]{2,1,0:T(8,128)(2,1)S(1)} %pad_maximum_fusion.6), channel_id=1, source_target_pairs={{0,3},{1,0},{2,1},{3,2},{4,7},{5,4},{6,5},{7,6},{8,11},{9,8},{10,9... | collective-permute-start | bytes 393224 | tf_op jit(solution)/shard_map/ppermute | solution.py:288
  26.4 32.6 %collective-permute-start.14 = (bf16[2,256,128]{2,1,0:T(8,128)(2,1)S(1)}, bf16[2,256,128]{2,1,0:T(8,128)(2,1)S(1)}, u32[]{:S(2)}, u32[]{:S(2)}) collective-permute-start(bf16[2,256,128]{2,1,0:T(8,128)(2,1)S(1)} %pad_maximum_fusion.6), channel_id=1, source_target_pairs={{0,2},{1,3},{2,0},{3,1},{4,6},{5,7},{6,4},{7,5},{8,10},{9,11},{10,... | collective-permute-start | bytes 393224 | tf_op jit(solution)/shard_map/ppermute | solution.py:288
  26.7 43.5 %collective-permute-start.5 = (bf16[4,2,272,128]{3,2,1,0:T(8,128)(2,1)S(1)}, bf16[4,2,272,128]{3,2,1,0:T(8,128)(2,1)}, u32[]{:S(2)}, u32[]{:S(2)}) collective-permute-start(bf16[4,2,272,128]{3,2,1,0:T(8,128)(2,1)S(1)} %pad_maximum_fusion.1.k0), channel_id=1, source_target_pairs={{0,2},{1,3},{2,0},{3,1},{4,6},{5,7},{6,4},{7,5},{8,10},{9,11},{10,... | collective-permute-start | bytes 1671176 | tf_op jit(solution)/shard_map/ppermute | solution.py:288
  29.9 43.3 %collective-permute-start.6 = (bf16[4,2,272,128]{3,2,1,0:T(8,128)(2,1)S(1)}, bf16[4,2,272,128]{3,2,1,0:T(8,128)(2,1)}, u32[]{:S(2)}, u32[]{:S(2)}) collective-permute-start(bf16[4,2,272,128]{3,2,1,0:T(8,128)(2,1)S(1)} %pad_maximum_fusion.1.k0), channel_id=1, source_target_pairs={{0,1},{1,2},{2,3},{3,0},{4,5},{5,6},{6,7},{7,4},{8,9},{9,10},{10,1... | collective-permute-start | bytes 1671176 | tf_op jit(solution)/shard_map/ppermute | solution.py:288
  31.3 46.5 %copy-start.7 = (f32[256]{0:T(256)S(1)}, f32[256]{0:T(256)}, u32[]{:S(2)}) copy-start(f32[256]{0:T(256)} %param.12) | copy-start | bytes 3076
  55.8 12.7 %collective-permute-start.7 = (bf16[256,512]{1,0:T(8,128)(2,1)S(1)}, bf16[256,512]{1,0:T(8,128)(2,1)S(1)}, u32[]{:S(2)}, u32[]{:S(2)}) collective-permute-start(bf16[256,512]{1,0:T(8,128)(2,1)S(1)} %get-tuple-element.45), channel_id=1, source_target_pairs={{0,15},{1,14},{2,13},{3,12},{4,11},{5,10},{6,9},{7,8},{8,7},{9,6},... | collective-permute-start | bytes 786440 | tf_op jit(solution)/shard_map/ppermute | solution.py:288
  59.0 6.3 %collective-permute-start.15 = (bf16[2,256,128]{2,1,0:T(8,128)(2,1)S(1)}, bf16[2,256,128]{2,1,0:T(8,128)(2,1)S(1)}, u32[]{:S(2)}, u32[]{:S(2)}) collective-permute-start(bf16[2,256,128]{2,1,0:T(8,128)(2,1)S(1)} %pad_maximum_fusion.6), channel_id=1, source_target_pairs={{0,1},{1,2},{2,3},{3,0},{4,5},{5,6},{6,7},{7,4},{8,9},{9,10},{10,1... | collective-permute-start | bytes 393224 | tf_op jit(solution)/shard_map/ppermute | solution.py:288
  65.3 87.8 %copy-start = (bf16[4,2,256,128]{3,2,1,0:T(8,128)(2,1)}, bf16[4,2,256,128]{3,2,1,0:T(8,128)(2,1)S(1)}, u32[]{:S(2)}) copy-start(bf16[4,2,256,128]{3,2,1,0:T(8,128)(2,1)S(1)} %pad_maximum_fusion.2.v0) | copy-start | bytes 1572868
  65.3 25.6 %collective-permute-start.16 = (bf16[4,2,256,128]{3,2,1,0:T(8,128)(2,1)S(1)}, bf16[4,2,256,128]{3,2,1,0:T(8,128)(2,1)}, u32[]{:S(2)}, u32[]{:S(2)}) collective-permute-start(bf16[4,2,256,128]{3,2,1,0:T(8,128)(2,1)S(1)} %pad_maximum_fusion.2.v0), channel_id=1, source_target_pairs={{0,12},{1,13},{2,14},{3,15},{4,0},{5,1},{6,2},{7,3},{8,4},{9,5},{1... | collective-permute-start | bytes 1572872 | tf_op jit(solution)/shard_map/ppermute | solution.py:288
  68.5 22.4 %collective-permute-start.17 = (bf16[4,2,256,128]{3,2,1,0:T(8,128)(2,1)S(1)}, bf16[4,2,256,128]{3,2,1,0:T(8,128)(2,1)}, u32[]{:S(2)}, u32[]{:S(2)}) collective-permute-start(bf16[4,2,256,128]{3,2,1,0:T(8,128)(2,1)S(1)} %pad_maximum_fusion.2.v0), channel_id=1, source_target_pairs={{0,8},{1,9},{2,10},{3,11},{4,12},{5,13},{6,14},{7,15},{8,0},{9,1},... | collective-permute-start | bytes 1572872 | tf_op jit(solution)/shard_map/ppermute | solution.py:288
  68.5 25.2 %collective-permute-start.18 = (bf16[4,2,256,128]{3,2,1,0:T(8,128)(2,1)S(1)}, bf16[4,2,256,128]{3,2,1,0:T(8,128)(2,1)}, u32[]{:S(2)}, u32[]{:S(2)}) collective-permute-start(bf16[4,2,256,128]{3,2,1,0:T(8,128)(2,1)S(1)} %pad_maximum_fusion.2.v0), channel_id=1, source_target_pairs={{0,4},{1,5},{2,6},{3,7},{4,8},{5,9},{6,10},{7,11},{8,12},{9,13},{1... | collective-permute-start | bytes 1572872 | tf_op jit(solution)/shard_map/ppermute | solution.py:288
  70.2 8.4 %collective-permute-start.8 = (bf16[256,512]{1,0:T(8,128)(2,1)S(1)}, bf16[256,512]{1,0:T(8,128)(2,1)S(1)}, u32[]{:S(2)}, u32[]{:S(2)}) collective-permute-start(bf16[256,512]{1,0:T(8,128)(2,1)S(1)} %get-tuple-element.47), channel_id=1, source_target_pairs={{0,16},{1,17},{2,18},{3,19},{4,20},{5,21},{6,22},{7,23},{8,24},{9,... | collective-permute-start | bytes 786440 | tf_op jit(solution)/shard_map/ppermute | solution.py:288
  73.2 12.3 %collective-permute-start.9 = (bf16[256,512]{1,0:T(8,128)(2,1)S(1)}, bf16[256,512]{1,0:T(8,128)(2,1)S(1)}, u32[]{:S(2)}, u32[]{:S(2)}) collective-permute-start(bf16[256,512]{1,0:T(8,128)(2,1)S(1)} %get-tuple-element.44), channel_id=1, source_target_pairs={{0,31},{1,30},{2,29},{3,28},{4,27},{5,26},{6,25},{7,24},{8,23},{9,... | collective-permute-start | bytes 786440 | tf_op jit(solution)/shard_map/ppermute | solution.py:288
  93.8 59.3 %copy-start.1 = (f32[512,128]{1,0:T(8,128)}, f32[512,128]{1,0:T(8,128)S(1)}, u32[]{:S(2)}) copy-start(f32[512,128]{1,0:T(8,128)S(1)} %broadcast_in_dim.44.w_ref) | copy-start | bytes 786436
  93.8 68.2 %copy-start.3 = (bf16[256,2048]{1,0:T(8,128)(2,1)S(1)}, bf16[256,2048]{1,0:T(8,128)(2,1)}, u32[]{:S(2)}) copy-start(bf16[256,2048]{1,0:T(8,128)(2,1)} %param.13) | copy-start | bytes 3145732
  158.7 12.3 %collective-permute-start.21 = (f32[4,256]{1,0:T(4,128)S(1)}, f32[4,256]{1,0:T(4,128)S(1)}, u32[]{:S(2)}, u32[]{:S(2)}) collective-permute-start(f32[4,256]{1,0:T(4,128)S(1)} %psum.7), channel_id=1, source_target_pairs={{0,31},{1,30},{2,29},{3,28},{4,27},{5,26},{6,25},{7,24},{8,23},{9,... | collective-permute-start | bytes 12296 | tf_op jit(solution)/shard_map/ppermute | solution.py:288
  162.1 19.5 %collective-permute-start.10 = (bf16[256,512]{1,0:T(8,128)(2,1)S(1)}, bf16[256,512]{1,0:T(8,128)(2,1)S(1)}, u32[]{:S(2)}, u32[]{:S(2)}) collective-permute-start(bf16[256,512]{1,0:T(8,128)(2,1)S(1)} %get-tuple-element.41), channel_id=1, source_target_pairs={{0,15},{1,14},{2,13},{3,12},{4,11},{5,10},{6,9},{7,8},{8,7},{9,6},... | collective-permute-start | bytes 786440 | tf_op jit(solution)/shard_map/ppermute | solution.py:288
  166.9 14.7 %collective-permute-start.11 = (bf16[256,512]{1,0:T(8,128)(2,1)S(1)}, bf16[256,512]{1,0:T(8,128)(2,1)S(1)}, u32[]{:S(2)}, u32[]{:S(2)}) collective-permute-start(bf16[256,512]{1,0:T(8,128)(2,1)S(1)} %get-tuple-element.43), channel_id=1, source_target_pairs={{0,16},{1,17},{2,18},{3,19},{4,20},{5,21},{6,22},{7,23},{8,24},{9,... | collective-permute-start | bytes 786440 | tf_op jit(solution)/shard_map/ppermute | solution.py:288
  167.3 14.3 %collective-permute-start.12 = (bf16[256,512]{1,0:T(8,128)(2,1)S(1)}, bf16[256,512]{1,0:T(8,128)(2,1)S(1)}, u32[]{:S(2)}, u32[]{:S(2)}) collective-permute-start(bf16[256,512]{1,0:T(8,128)(2,1)S(1)} %get-tuple-element.40), channel_id=1, source_target_pairs={{0,31},{1,30},{2,29},{3,28},{4,27},{5,26},{6,25},{7,24},{8,23},{9,... | collective-permute-start | bytes 786440 | tf_op jit(solution)/shard_map/ppermute | solution.py:288
  170.5 11.0 %collective-permute-start.20 = (f32[4,256]{1,0:T(4,128)S(1)}, f32[4,256]{1,0:T(4,128)S(1)}, u32[]{:S(2)}, u32[]{:S(2)}) collective-permute-start(f32[4,256]{1,0:T(4,128)S(1)} %psum.7), channel_id=1, source_target_pairs={{0,16},{1,17},{2,18},{3,19},{4,20},{5,21},{6,22},{7,23},{8,24},{9,... | collective-permute-start | bytes 12296 | tf_op jit(solution)/shard_map/ppermute | solution.py:288
  171.0 10.5 %collective-permute-start.19 = (f32[4,256]{1,0:T(4,128)S(1)}, f32[4,256]{1,0:T(4,128)S(1)}, u32[]{:S(2)}, u32[]{:S(2)}) collective-permute-start(f32[4,256]{1,0:T(4,128)S(1)} %psum.7), channel_id=1, source_target_pairs={{0,15},{1,14},{2,13},{3,12},{4,11},{5,10},{6,9},{7,8},{8,7},{9,6},... | collective-permute-start | bytes 12296 | tf_op jit(solution)/shard_map/ppermute | solution.py:288
  181.6 0.7 copy-start.10
  181.6 0.8 copy-start.11
  237.6 48.6 %copy-start.9 = (bf16[4,2,256,128]{3,2,1,0:T(8,128)(2,1)S(1)}, bf16[4,2,256,128]{3,2,1,0:T(8,128)(2,1)}, u32[]{:S(2)}) copy-start(bf16[4,2,256,128]{3,2,1,0:T(8,128)(2,1)} %get-tuple-element.30) | copy-start | bytes 1572868
  237.8 11.3 %collective-permute-start.38 = (f32[4,512]{1,0:T(4,128)S(1)}, f32[4,512]{1,0:T(4,128)S(1)}, u32[]{:S(2)}, u32[]{:S(2)}) collective-permute-start(f32[4,512]{1,0:T(4,128)S(1)} %dynamic_update_slice.5), channel_id=1, source_target_pairs={{0,3},{1,0},{2,1},{3,2},{4,7},{5,4},{6,5},{7,6},{8,11},{9,8},{10,9... | collective-permute-start | bytes 24584 | tf_op jit(solution)/shard_map/ppermute | solution.py:288
  237.9 11.2 %collective-permute-start.39 = (f32[4,512]{1,0:T(4,128)S(1)}, f32[4,512]{1,0:T(4,128)S(1)}, u32[]{:S(2)}, u32[]{:S(2)}) collective-permute-start(f32[4,512]{1,0:T(4,128)S(1)} %dynamic_update_slice.5), channel_id=1, source_target_pairs={{0,2},{1,3},{2,0},{3,1},{4,6},{5,7},{6,4},{7,5},{8,10},{9,11},{10,... | collective-permute-start | bytes 24584 | tf_op jit(solution)/shard_map/ppermute | solution.py:288
  241.7 7.4 %collective-permute-start.40 = (f32[4,512]{1,0:T(4,128)S(1)}, f32[4,512]{1,0:T(4,128)S(1)}, u32[]{:S(2)}, u32[]{:S(2)}) collective-permute-start(f32[4,512]{1,0:T(4,128)S(1)} %dynamic_update_slice.5), channel_id=1, source_target_pairs={{0,1},{1,2},{2,3},{3,0},{4,5},{5,6},{6,7},{7,4},{8,9},{9,10},{10,1... | collective-permute-start | bytes 24584 | tf_op jit(solution)/shard_map/ppermute | solution.py:288
  243.7 20.3 %collective-permute-start.22 = (bf16[256,512]{1,0:T(8,128)(2,1)S(1)}, bf16[256,512]{1,0:T(8,128)(2,1)S(1)}, u32[]{:S(2)}, u32[]{:S(2)}) collective-permute-start(bf16[256,512]{1,0:T(8,128)(2,1)S(1)} %get-tuple-element.39), channel_id=1, source_target_pairs={{0,31},{1,30},{2,29},{3,28},{4,27},{5,26},{6,25},{7,24},{8,23},{9,... | collective-permute-start | bytes 786440 | tf_op jit(solution)/shard_map/ppermute | solution.py:288
  249.2 3.7 %collective-permute-start.41 = (f32[4,512]{1,0:T(4,128)S(1)}, f32[4,512]{1,0:T(4,128)S(1)}, u32[]{:S(2)}, u32[]{:S(2)}) collective-permute-start(f32[4,512]{1,0:T(4,128)S(1)} %add_add_fusion.1), channel_id=1, source_target_pairs={{0,12},{1,13},{2,14},{3,15},{4,0},{5,1},{6,2},{7,3},{8,4},{9,5},{1... | collective-permute-start | bytes 24584 | tf_op jit(solution)/shard_map/ppermute | solution.py:288
  250.6 5.3 %collective-permute-start.42 = (f32[4,512]{1,0:T(4,128)S(1)}, f32[4,512]{1,0:T(4,128)S(1)}, u32[]{:S(2)}, u32[]{:S(2)}) collective-permute-start(f32[4,512]{1,0:T(4,128)S(1)} %add_add_fusion.1), channel_id=1, source_target_pairs={{0,8},{1,9},{2,10},{3,11},{4,12},{5,13},{6,14},{7,15},{8,0},{9,1},... | collective-permute-start | bytes 24584 | tf_op jit(solution)/shard_map/ppermute | solution.py:288
  250.7 5.5 %collective-permute-start.43 = (f32[4,512]{1,0:T(4,128)S(1)}, f32[4,512]{1,0:T(4,128)S(1)}, u32[]{:S(2)}, u32[]{:S(2)}) collective-permute-start(f32[4,512]{1,0:T(4,128)S(1)} %add_add_fusion.1), channel_id=1, source_target_pairs={{0,4},{1,5},{2,6},{3,7},{4,8},{5,9},{6,10},{7,11},{8,12},{9,13},{1... | collective-permute-start | bytes 24584 | tf_op jit(solution)/shard_map/ppermute | solution.py:288
  256.1 5.5 %collective-permute-start.44 = (f32[4,512]{1,0:T(4,128)S(1)}, f32[4,512]{1,0:T(4,128)S(1)}, u32[]{:S(2)}, u32[]{:S(2)}) collective-permute-start(f32[4,512]{1,0:T(4,128)S(1)} %add_add_fusion), channel_id=1, source_target_pairs={{0,16},{1,17},{2,18},{3,19},{4,20},{5,21},{6,22},{7,23},{8,24},{9,... | collective-permute-start | bytes 24584 | tf_op jit(solution)/shard_map/ppermute | solution.py:288
  258.4 32.0 %collective-permute-start.25 = (bf16[4,2,256,128]{3,2,1,0:T(8,128)(2,1)}, bf16[4,2,256,128]{3,2,1,0:T(8,128)(2,1)S(1)}, u32[]{:S(2)}, u32[]{:S(2)}) collective-permute-start(bf16[4,2,256,128]{3,2,1,0:T(8,128)(2,1)} %get-tuple-element.25), channel_id=1, source_target_pairs={{0,1},{1,2},{2,3},{3,0},{4,5},{5,6},{6,7},{7,4},{8,9},{9,10},{10,1... | collective-permute-start | bytes 1572872 | tf_op jit(solution)/shard_map/ppermute | solution.py:288
  258.4 33.0 %collective-permute-start.26 = (bf16[4,2,256,128]{3,2,1,0:T(8,128)(2,1)}, bf16[4,2,256,128]{3,2,1,0:T(8,128)(2,1)S(1)}, u32[]{:S(2)}, u32[]{:S(2)}) collective-permute-start(bf16[4,2,256,128]{3,2,1,0:T(8,128)(2,1)} %get-tuple-element.26), channel_id=1, source_target_pairs={{0,2},{1,3},{2,0},{3,1},{4,6},{5,7},{6,4},{7,5},{8,10},{9,11},{10,... | collective-permute-start | bytes 1572872 | tf_op jit(solution)/shard_map/ppermute | solution.py:288
  260.4 30.9 %collective-permute-start.27 = (bf16[4,2,256,128]{3,2,1,0:T(8,128)(2,1)}, bf16[4,2,256,128]{3,2,1,0:T(8,128)(2,1)S(1)}, u32[]{:S(2)}, u32[]{:S(2)}) collective-permute-start(bf16[4,2,256,128]{3,2,1,0:T(8,128)(2,1)} %get-tuple-element.27), channel_id=1, source_target_pairs={{0,3},{1,0},{2,1},{3,2},{4,7},{5,4},{6,5},{7,6},{8,11},{9,8},{10,9... | collective-permute-start | bytes 1572872 | tf_op jit(solution)/shard_map/ppermute | solution.py:288
  261.6 24.6 %collective-permute-start.23 = (bf16[256,512]{1,0:T(8,128)(2,1)S(1)}, bf16[256,512]{1,0:T(8,128)(2,1)S(1)}, u32[]{:S(2)}, u32[]{:S(2)}) collective-permute-start(bf16[256,512]{1,0:T(8,128)(2,1)S(1)} %get-tuple-element.37), channel_id=1, source_target_pairs={{0,15},{1,14},{2,13},{3,12},{4,11},{5,10},{6,9},{7,8},{8,7},{9,6},... | collective-permute-start | bytes 786440 | tf_op jit(solution)/shard_map/ppermute | solution.py:288
  263.9 22.3 %collective-permute-start.24 = (bf16[256,512]{1,0:T(8,128)(2,1)S(1)}, bf16[256,512]{1,0:T(8,128)(2,1)S(1)}, u32[]{:S(2)}, u32[]{:S(2)}) collective-permute-start(bf16[256,512]{1,0:T(8,128)(2,1)S(1)} %get-tuple-element.38), channel_id=1, source_target_pairs={{0,16},{1,17},{2,18},{3,19},{4,20},{5,21},{6,22},{7,23},{8,24},{9,... | collective-permute-start | bytes 786440 | tf_op jit(solution)/shard_map/ppermute | solution.py:288
  286.2 27.0 %collective-permute-start.31 = (bf16[4,2,256,128]{3,2,1,0:T(8,128)(2,1)}, bf16[4,2,256,128]{3,2,1,0:T(8,128)(2,1)S(1)}, u32[]{:S(2)}, u32[]{:S(2)}) collective-permute-start(bf16[4,2,256,128]{3,2,1,0:T(8,128)(2,1)} %get-tuple-element.29), channel_id=1, source_target_pairs={{0,4},{1,5},{2,6},{3,7},{4,8},{5,9},{6,10},{7,11},{8,12},{9,13},{1... | collective-permute-start | bytes 1572872 | tf_op jit(solution)/shard_map/ppermute | solution.py:288
  286.3 4.1 %copy-start.8 = (bf16[4,2,256,128]{3,2,1,0:T(8,128)(2,1)S(1)}, bf16[4,2,256,128]{3,2,1,0:T(8,128)(2,1)}, u32[]{:S(2)}) copy-start(bf16[4,2,256,128]{3,2,1,0:T(8,128)(2,1)} %get-tuple-element.31) | copy-start | bytes 1572868
  286.3 5.1 %copy-start.6 = (bf16[4,2,256,128]{3,2,1,0:T(8,128)(2,1)S(1)}, bf16[4,2,256,128]{3,2,1,0:T(8,128)(2,1)}, u32[]{:S(2)}) copy-start(bf16[4,2,256,128]{3,2,1,0:T(8,128)(2,1)} %get-tuple-element.24) | copy-start | bytes 1572868
  286.3 26.9 %collective-permute-start.32 = (bf16[4,2,256,128]{3,2,1,0:T(8,128)(2,1)S(1)}, bf16[4,2,256,128]{3,2,1,0:T(8,128)(2,1)S(1)}, u32[]{:S(2)}, u32[]{:S(2)}) collective-permute-start(bf16[4,2,256,128]{3,2,1,0:T(8,128)(2,1)S(1)} %copy-done.9), channel_id=1, source_target_pairs={{0,8},{1,9},{2,10},{3,11},{4,12},{5,13},{6,14},{7,15},{8,0},{9,1},... | collective-permute-start | bytes 1572872 | tf_op jit(solution)/shard_map/ppermute | solution.py:288
  290.4 23.3 %collective-permute-start.33 = (bf16[4,2,256,128]{3,2,1,0:T(8,128)(2,1)S(1)}, bf16[4,2,256,128]{3,2,1,0:T(8,128)(2,1)S(1)}, u32[]{:S(2)}, u32[]{:S(2)}) collective-permute-start(bf16[4,2,256,128]{3,2,1,0:T(8,128)(2,1)S(1)} %copy-done.8), channel_id=1, source_target_pairs={{0,12},{1,13},{2,14},{3,15},{4,0},{5,1},{6,2},{7,3},{8,4},{9,5},{1... | collective-permute-start | bytes 1572872 | tf_op jit(solution)/shard_map/ppermute | solution.py:288
  291.7 22.0 %copy-start.5 = (bf16[4,2,256,128]{3,2,1,0:T(8,128)(2,1)S(1)}, bf16[4,2,256,128]{3,2,1,0:T(8,128)(2,1)}, u32[]{:S(2)}) copy-start(bf16[4,2,256,128]{3,2,1,0:T(8,128)(2,1)} %get-tuple-element.28) | copy-start | bytes 1572868
  291.7 27.9 %collective-permute-start.28 = (bf16[2,256,128]{2,1,0:T(8,128)(2,1)S(1)}, bf16[2,256,128]{2,1,0:T(8,128)(2,1)S(1)}, u32[]{:S(2)}, u32[]{:S(2)}) collective-permute-start(bf16[2,256,128]{2,1,0:T(8,128)(2,1)S(1)} %get-tuple-element.48), channel_id=1, source_target_pairs={{0,4},{1,5},{2,6},{3,7},{4,8},{5,9},{6,10},{7,11},{8,12},{9,13},{1... | collective-permute-start | bytes 393224 | tf_op jit(solution)/shard_map/ppermute | solution.py:288
  292.9 26.8 %collective-permute-start.29 = (bf16[2,256,128]{2,1,0:T(8,128)(2,1)S(1)}, bf16[2,256,128]{2,1,0:T(8,128)(2,1)S(1)}, u32[]{:S(2)}, u32[]{:S(2)}) collective-permute-start(bf16[2,256,128]{2,1,0:T(8,128)(2,1)S(1)} %get-tuple-element.50), channel_id=1, source_target_pairs={{0,8},{1,9},{2,10},{3,11},{4,12},{5,13},{6,14},{7,15},{8,0},{9,1},... | collective-permute-start | bytes 393224 | tf_op jit(solution)/shard_map/ppermute | solution.py:288
  313.2 6.5 %collective-permute-start.30 = (bf16[2,256,128]{2,1,0:T(8,128)(2,1)S(1)}, bf16[2,256,128]{2,1,0:T(8,128)(2,1)S(1)}, u32[]{:S(2)}, u32[]{:S(2)}) collective-permute-start(bf16[2,256,128]{2,1,0:T(8,128)(2,1)S(1)} %get-tuple-element.49), channel_id=1, source_target_pairs={{0,12},{1,13},{2,14},{3,15},{4,0},{5,1},{6,2},{7,3},{8,4},{9,5},{1... | collective-permute-start | bytes 393224 | tf_op jit(solution)/shard_map/ppermute | solution.py:288
  314.0 8.3 %collective-permute-start.34 = (bf16[2,256,128]{2,1,0:T(8,128)(2,1)S(1)}, bf16[2,256,128]{2,1,0:T(8,128)(2,1)S(1)}, u32[]{:S(2)}, u32[]{:S(2)}) collective-permute-start(bf16[2,256,128]{2,1,0:T(8,128)(2,1)S(1)} %get-tuple-element.51), channel_id=1, source_target_pairs={{0,1},{1,2},{2,3},{3,0},{4,5},{5,6},{6,7},{7,4},{8,9},{9,10},{10,1... | collective-permute-start | bytes 393224 | tf_op jit(solution)/shard_map/ppermute | solution.py:288
  315.8 8.2 %collective-permute-start.35 = (bf16[2,256,128]{2,1,0:T(8,128)(2,1)S(1)}, bf16[2,256,128]{2,1,0:T(8,128)(2,1)S(1)}, u32[]{:S(2)}, u32[]{:S(2)}) collective-permute-start(bf16[2,256,128]{2,1,0:T(8,128)(2,1)S(1)} %get-tuple-element.53), channel_id=1, source_target_pairs={{0,2},{1,3},{2,0},{3,1},{4,6},{5,7},{6,4},{7,5},{8,10},{9,11},{10,... | collective-permute-start | bytes 393224 | tf_op jit(solution)/shard_map/ppermute | solution.py:288
  319.6 5.0 %collective-permute-start.36 = (bf16[2,256,128]{2,1,0:T(8,128)(2,1)S(1)}, bf16[2,256,128]{2,1,0:T(8,128)(2,1)S(1)}, u32[]{:S(2)}, u32[]{:S(2)}) collective-permute-start(bf16[2,256,128]{2,1,0:T(8,128)(2,1)S(1)} %get-tuple-element.52), channel_id=1, source_target_pairs={{0,3},{1,0},{2,1},{3,2},{4,7},{5,4},{6,5},{7,6},{8,11},{9,8},{10,9... | collective-permute-start | bytes 393224 | tf_op jit(solution)/shard_map/ppermute | solution.py:288
  324.7 6.6 %collective-permute-start.37 = (bf16[256,256]{1,0:T(8,128)(2,1)S(1)}, bf16[256,256]{1,0:T(8,128)(2,1)S(1)}, u32[]{:S(2)}, u32[]{:S(2)}) collective-permute-start(bf16[256,256]{1,0:T(8,128)(2,1)S(1)} %select_bitcast_fusion.2), channel_id=1, source_target_pairs={{0,16},{1,17},{2,18},{3,19},{4,20},{5,21},{6,22},{7,23},{8,24},{9,... | collective-permute-start | bytes 393224 | tf_op jit(solution)/shard_map/ppermute | solution.py:288
